TPU v7x, 32 devices: a whole 2x2x4 slice. The times are simulated.
32 devices in a mesh: row: 4 (over y, core), col: 8 (over z, x).
Axes of the slice: x: 2, y: 2, z: 4, core: 2. Of those that a mesh axis runs over, the one named last changes fastest.
Arguments:
- transition: bfloat16 [32768, 32768], P('row', 'col'), may hold values from 1.5258789e-06 to 0.0024414062, as said below
- emission: bfloat16 [96, 32768], P(None, 'col'), may hold values from 0.0099487305 to 1
- token_ids: int32 [2, 192], replicated, may hold values from 0 to 95
- forward: bfloat16 [2, 192, 32768], P(None, 'col', 'row'), may hold values from 3.0517578e-06 to 0.0008239746, as said below
- backward_last: float32 [192, 32768], P('row', 'col'), may hold values from 0.1 to 10
Outputs:
- backward: float32 [2, 192, 32768], P(None, 'col', 'row')
- counts: float32 [32768, 1024], P('row', 'col')
Inputs may be any that keep to these rules, and one draw needn't show every extreme that they name: Positive transition weights. Positive forward weights.
All inputs are finite; a program needn't handle non-finite values.
Results may differ from a plain program's by a relative error of at most 0.00048.
Values may be sent and summed in bfloat16 or wider, within the bound.
A program may use at most 192 MiB of HBM per device.

v0:
```python
import jax
import jax.numpy as jnp
from jax import lax
from jax.sharding import PartitionSpec as P

H = 32768
N = 192
DW = 128


def spread(value, axis, source):
    kept = jnp.where(lax.axis_index(axis) == source, value, 0).astype(value.dtype)
    return lax.psum(kept, axis)


def on_device(transition, emission, token_ids, forward, backward_last):
    row_count = lax.axis_size("row")
    col_count = lax.axis_size("col")
    col_index = lax.axis_index("col")
    ratio = col_count // row_count
    local_seqs = forward.shape[1]
    block_src = transition.shape[0]
    block_dst = transition.shape[1]
    seq_total = local_seqs * col_count
    forward_all = lax.all_gather(forward, "col", axis=1, tiled=True)
    backward_next = lax.all_gather(backward_last, "row", axis=0, tiled=True)
    columns = lax.broadcasted_iota(jnp.int32, (seq_total, emission.shape[0]), 1)
    window = transition[:, :DW]
    totals = jnp.zeros((block_src, DW), jnp.float32)
    outputs = [None, None]
    for step in (1, 0):
        onehot = (token_ids[step][:, None] == columns).astype(jnp.bfloat16)
        emitted = jnp.dot(onehot, emission, preferred_element_type=jnp.float32)
        weighted_back = (emitted * backward_next).astype(jnp.bfloat16)
        partial_value = lax.dot_general(
            weighted_back, transition, (((1,), (1,)), ((), ())), preferred_element_type=jnp.float32
        )
        alpha_all = forward_all[step].astype(jnp.float32)
        summed = lax.psum(partial_value, "col")
        mine = lax.dynamic_slice_in_dim(summed, col_index * local_seqs, local_seqs, 0)
        alpha_mine = forward[step].astype(jnp.float32)
        local_norm = lax.psum(jnp.sum(alpha_mine * mine, axis=1), "row")
        normal_all = lax.all_gather(local_norm, "col", axis=0, tiled=True)
        normal_mine = lax.dynamic_slice_in_dim(normal_all, col_index * local_seqs, local_seqs, 0)
        outputs[step] = mine / normal_mine[:, None]
        scaled = (alpha_all / normal_all[:, None]).astype(jnp.bfloat16)
        totals = totals + lax.dot_general(
            scaled,
            weighted_back[:, :DW],
            (((0,), (0,)), ((), ())),
            preferred_element_type=jnp.float32,
        )
        if step == 1:
            whole = summed / normal_all[:, None]
            piece = lax.dynamic_slice_in_dim(whole, col_index % ratio * block_dst, block_dst, 1)
            backward_next = spread(piece, "row", col_index // ratio)
    counts = window.astype(jnp.float32) * totals * (H * H / N)
    return (jnp.stack(outputs), counts)


def solution(mesh):
    in_specs = (P("row", "col"), P(None, "col"), P(), P(None, "col", "row"), P("row", "col"))
    out_specs = (P(None, "col", "row"), P("row", "col"))
    return jax.shard_map(
        on_device, mesh=mesh, in_specs=in_specs, out_specs=out_specs, check_vma=False
    )
```

profile of v0, /device:TPU:0, one launch (start us, length us, event | category | flops | bytes accessed | tf_op | source)
XLA Modules:
  0.0 741.6 jit_solution(9007567216397277755)
XLA Ops:
  7.2 0.0 copy-start
  7.2 0.0 all-gather.3.cloned.1.call-start
  7.2 0.7 all-gather.3.cloned.1.call-update
  7.9 0.0 all-reduce.6.cloned.1.call-start
  8.0 0.8 fusion.17
  8.7 32.1 %all-gather.3.cloned.1.call-done = f32[192,4096]{1,0:T(8,128)} async-done(((f32[48,4096]{1,0:T(8,128)}), f32[192,4096]{1,0:T(8,128)}) %all-gather.3.cloned.1.call-update) | async-done | bytes 3145744 | tf_op jit(solution)/shard_map/all_gather | solution.py:26
  40.8 0.0 copy-done
  40.8 2.5 fusion.5
  43.3 31.1 %fusion.18 = f32[192,8192]{1,0:T(8,128)} fusion(bf16[192,4096]{1,0:T(8,128)(2,1)S(1)} %fusion.5, bf16[8192,4096]{1,0:T(8,128)(2,1)} %param.5), kind=kOutput, calls=%fused_computation.31 | convolution fusion | flops 12884901888 | bytes 74973184 | tf_op jit(solution)/shard_map/dot_general | solution.py:35
  74.5 0.0 copy-start.3
  74.5 0.0 copy-start.1
  74.5 0.0 all-reduce.6.cloned.1.call-update
  74.5 0.0 all-reduce.8.cloned.1.call-start
  74.6 0.6 copy-done.3
  75.1 0.6 dynamic-slice
  76.4 209.8 %all-reduce.6.cloned.1.call-done = f32[192,8192]{1,0:T(8,128)} async-done(((f32[192,8192]{1,0:T(8,128)}), f32[192,8192]{1,0:T(8,128)}) %all-reduce.6.cloned.1.call-update) | async-done | bytes 6291472 | tf_op jit(solution)/shard_map/psum | solution.py:39
  286.2 0.0 copy-done.1
  286.2 1.3 fusion.12
  287.5 6.9 psum.36
  294.4 0.2 dynamic-update-slice
  294.7 19.4 %all-reduce = f32[192]{0:T(256)S(1)} all-reduce(f32[192]{0:T(256)S(1)} %dynamic-update-slice), channel_id=1, replica_groups=mesh['row'=4,'col'=8] {'col'}, use_global_device_ids=true, to_apply=%add | all-reduce | flops 192 | bytes 1536
  314.1 4.0 fusion.7
  318.1 0.0 all-reduce.8.cloned.1.call-update
  318.1 0.0 all-gather.5.cloned.1.call-start
  318.1 0.5 all-gather.5.cloned.1.call-update
  318.7 0.0 all-reduce.10.cloned.1.call-start
  318.7 64.3 %all-reduce.8.cloned.1.call-done = f32[192,4096]{1,0:T(8,128)} async-done(((f32[192,4096]{1,0:T(8,128)}), f32[192,4096]{1,0:T(8,128)}) %all-reduce.8.cloned.1.call-update) | async-done | bytes 3145744 | tf_op jit(solution)/shard_map/psum | solution.py:13
  383.0 3.7 fusion.4
  386.7 30.8 %fusion.19 = f32[192,8192]{1,0:T(8,128)} fusion(bf16[192,4096]{1,0:T(8,128)(2,1)} %fusion.4, bf16[8192,4096]{1,0:T(8,128)(2,1)} %param.5), kind=kOutput, calls=%fused_computation.32 | convolution fusion | flops 12884901888 | bytes 74973184 | tf_op jit(solution)/shard_map/dot_general | solution.py:35
  417.5 0.0 all-reduce.10.cloned.1.call-update
  417.5 0.1 dynamic_slice.19
  417.6 0.0 copy-start.2
  417.6 66.8 %all-gather.5.cloned.1.call-done = bf16[2,192,8192]{2,1,0:T(8,128)(2,1)} async-done(((bf16[2,24,8192]{2,1,0:T(8,128)(2,1)}), bf16[2,192,8192]{2,1,0:T(8,128)(2,1)}) %all-gather.5.cloned.1.call-update) | async-done | bytes 6291472 | tf_op jit(solution)/shard_map/all_gather | solution.py:25
  484.4 5.4 fusion.9
  489.9 1.3 divide_bitcast_fusion
  491.1 207.2 %all-reduce.10.cloned.1.call-done = f32[192,8192]{1,0:T(8,128)} async-done(((f32[192,8192]{1,0:T(8,128)}), f32[192,8192]{1,0:T(8,128)}) %all-reduce.10.cloned.1.call-update) | async-done | bytes 6291472 | tf_op jit(solution)/shard_map/psum | solution.py:39
  698.3 0.0 copy-done.2
  698.3 1.3 fusion.11
  699.6 6.9 psum.39
  706.5 0.2 dynamic-update-slice.1
  706.7 19.4 %all-reduce.1 = f32[192]{0:T(256)S(1)} all-reduce(f32[192]{0:T(256)S(1)} %dynamic-update-slice.1), channel_id=1, replica_groups=mesh['row'=4,'col'=8] {'col'}, use_global_device_ids=true, to_apply=%add.1 | all-reduce | flops 192 | bytes 1536
  726.1 0.0 copy-start.4
  726.2 0.1 dynamic_slice.18
  726.2 1.4 divide_bitcast_fusion.1
  727.6 1.2 pad_maximum_fusion
  728.9 0.0 copy-done.4
  728.9 6.2 fusion.1
  (2 shorter events, 0.0 us)
Async XLA Ops:
  7.2 33.7 %copy-start = (bf16[96,4096]{1,0:T(8,128)(2,1)S(1)}, bf16[96,4096]{1,0:T(8,128)(2,1)}, u32[]{:S(2)}) copy-start(bf16[96,4096]{1,0:T(8,128)(2,1)} %param.6) | copy-start | bytes 2359300
  7.2 33.7 %all-gather.3.cloned.1.call-start = ((), (), s32[]{:S(2)}) async-start(), calls=%async_computation | async-start | bytes 3932160 | tf_op jit(solution)/shard_map/all_gather | solution.py:26
  7.9 278.3 %all-reduce.6.cloned.1.call-start = ((), (), s32[]{:S(2)}) async-start(), calls=%async_computation.1 | async-start | bytes 12582912 | tf_op jit(solution)/shard_map/psum | solution.py:39
  74.5 0.7 copy-start.3
  74.5 211.8 %copy-start.1 = (bf16[2,24,8192]{2,1,0:T(8,128)(2,1)S(1)}, bf16[2,24,8192]{2,1,0:T(8,128)(2,1)}, u32[]{:S(2)}) copy-start(bf16[2,24,8192]{2,1,0:T(8,128)(2,1)} %param.8) | copy-start | bytes 2359300
  74.5 308.5 %all-reduce.8.cloned.1.call-start = ((), (), s32[]{:S(2)}) async-start(), calls=%async_computation.2 | async-start | bytes 6291456 | tf_op jit(solution)/shard_map/psum | solution.py:13
  318.1 166.4 %all-gather.5.cloned.1.call-start = ((), (), s32[]{:S(2)}) async-start(), calls=%async_computation.4 | async-start | bytes 7077888 | tf_op jit(solution)/shard_map/all_gather | solution.py:25
  318.7 379.7 %all-reduce.10.cloned.1.call-start = ((), (), s32[]{:S(2)}) async-start(), calls=%async_computation.3 | async-start | bytes 12582912 | tf_op jit(solution)/shard_map/psum | solution.py:39
  417.6 280.7 %copy-start.2 = (bf16[2,24,8192]{2,1,0:T(8,128)(2,1)S(1)}, bf16[2,24,8192]{2,1,0:T(8,128)(2,1)}, u32[]{:S(2)}) copy-start(bf16[2,24,8192]{2,1,0:T(8,128)(2,1)} %param.8) | copy-start | bytes 2359300
  726.1 2.7 copy-start.4
Sparse Core Ops, SparseCore 0:
  9.6 31.2 all-gather.2
  74.6 211.5 all-reduce.5
  318.2 64.7 all-reduce.7
  385.3 99.1 all-gather.4
  488.5 209.7 all-reduce.9
where the time goes:
time: 742 us
  waiting for transfers between devices  582 us (78%)
  matrix products  79.7 us (11%)
  blocking collectives  52.5 us (7%)
  between operations  14.5 us (2%)
  other arithmetic  10.5 us (1%)
    psum x2, waiting for transfers between devices, on_device(): summed = lax.psum(partial_value, 'col')  417 us
    all_gather x1, waiting for transfers between devices, on_device(): forward_all = lax.all_gather(forward, 'col', axis=1, tiled=True)  66.8 us
    psum x1, waiting for transfers between devices, spread(): return lax.psum(kept, axis)  64.3 us
    dot_general x2, matrix products, on_device(): lax.dot_general(weighted_back, transition, (((1,), (1,)), ((), ())), pref...  61.9 us
    unnamed x2, blocking collectives  38.8 us
    all_gather x1, waiting for transfers between devices, on_device(): backward_next = lax.all_gather(backward_last, 'row', axis=0, tiled=True)  32.1 us
  transfers between devices with their start and end apart: 5, of which 5 were waited for; matrix products, arithmetic and copies ran while one was open for 6% of the time, Pallas kernels for 0%

commit v1 on v0

--- a/solution.py
+++ b/solution.py
@@ -6,6 +6,20 @@
 H = 32768
 N = 192
 DW = 128
+
+
+def _create_tails(content):
+    world = lax.psum(1, "col")
+
+    def switch_the_unit(far_arr, extra):
+        if extra >= world:
+            return far_arr
+        return switch_the_unit(
+            far_arr + lax.ppermute(far_arr, "col", [(c, c ^ extra) for c in range(world)]),
+            2 * extra,
+        )
+
+    return switch_the_unit(content, 1)
 
 
 def spread(value, axis, source):
@@ -36,7 +50,7 @@
             weighted_back, transition, (((1,), (1,)), ((), ())), preferred_element_type=jnp.float32
         )
         alpha_all = forward_all[step].astype(jnp.float32)
-        summed = lax.psum(partial_value, "col")
+        summed = _create_tails(partial_value)
         mine = lax.dynamic_slice_in_dim(summed, col_index * local_seqs, local_seqs, 0)
         alpha_mine = forward[step].astype(jnp.float32)
         local_norm = lax.psum(jnp.sum(alpha_mine * mine, axis=1), "row")

time: 742 us -> 1410 us (1.90)
  waiting for transfers between devices: 582 us -> 1210 us
  other arithmetic: 10.5 us -> 35 us
    ppermute x0 -> x6, waiting for transfers between devices: none -> 1120 us  [switch_the_unit(): lax.ppermute(far_arr, 'col', [(c, c ^ extra) for c in range(world)])]
    psum x2 -> x0, waiting for transfers between devices: 417 us -> none  [on_device(): summed = lax.psum(partial_value, 'col')]
    all_gather x1, waiting for transfers between devices: 66.8 us -> 0.01 us  [on_device(): forward_all = lax.all_gather(forward, 'col', axis=1, tiled=True)]
    add x0 -> x5, other arithmetic: none -> 20.7 us  [switch_the_unit(): far_arr + lax.ppermute(far_arr, 'col', [(c, c ^ extra) for c in range(wor...]
  transfers between devices with their start and end apart: 5 -> 9, of which waited for: 5 -> 8; matrix products, arithmetic and copies ran while one was open for 6% -> 1% of each run, Pallas kernels for 0% -> 0%
where the time goes in v1:
time: 1410 us
  waiting for transfers between devices  1210 us (86%)
  matrix products  78.3 us (6%)
  blocking collectives  55.3 us (4%)
  other arithmetic  35 us (2%)
  between operations  16.2 us (1%)
    ppermute x6, waiting for transfers between devices, switch_the_unit(): lax.ppermute(far_arr, 'col', [(c, c ^ extra) for c in range(world)])  1120 us
    psum x1, waiting for transfers between devices, spread(): return lax.psum(kept, axis)  63.4 us
    dot_general x2, matrix products, on_device(): lax.dot_general(weighted_back, transition, (((1,), (1,)), ((), ())), pref...  61.8 us
    unnamed x2, blocking collectives  43.8 us
    all_gather x1, waiting for transfers between devices, on_device(): backward_next = lax.all_gather(backward_last, 'row', axis=0, tiled=True)  32.1 us
  transfers between devices with their start and end apart: 9, of which 8 were waited for; matrix products, arithmetic and copies ran while one was open for 1% of the time, Pallas kernels for 0%

profile of v1, /device:TPU:0, one launch (start us, length us, event | category | flops | bytes accessed | tf_op | source)
XLA Modules:
  0.0 1411.9 jit_solution(18185076657245575194)
XLA Ops:
  8.0 0.0 copy-start
  8.0 0.0 all-gather.3.cloned.1.call-start
  8.1 0.7 all-gather.3.cloned.1.call-update
  8.7 0.0 all-reduce.4.cloned.1.call-start
  8.8 0.8 fusion.17
  9.6 32.1 %all-gather.3.cloned.1.call-done = f32[192,4096]{1,0:T(8,128)} async-done(((f32[48,4096]{1,0:T(8,128)}), f32[192,4096]{1,0:T(8,128)}) %all-gather.3.cloned.1.call-update) | async-done | bytes 3145744 | tf_op jit(solution)/shard_map/all_gather | solution.py:40
  41.7 0.0 copy-done
  41.7 2.5 fusion.4
  44.2 31.1 %fusion.18 = f32[192,8192]{1,0:T(8,128)} fusion(bf16[192,4096]{1,0:T(8,128)(2,1)S(1)} %fusion.4, bf16[8192,4096]{1,0:T(8,128)(2,1)} %param.5), kind=kOutput, calls=%fused_computation.32 | convolution fusion | flops 12884901888 | bytes 74973184 | tf_op jit(solution)/shard_map/dot_general | solution.py:49
  75.3 1.5 collective-permute-start
  76.8 136.4 %collective-permute-done = f32[192,8192]{1,0:T(8,128)S(1)} collective-permute-done((f32[192,8192]{1,0:T(8,128)}, f32[192,8192]{1,0:T(8,128)S(1)}, u32[]{:S(2)}, u32[]{:S(2)}) %collective-permute-start) | collective-permute-done | bytes 6291488 | tf_op jit(solution)/shard_map/ppermute | solution.py:18
  213.2 3.6 add.41
  216.8 0.0 copy-start.5
  216.8 1.6 collective-permute-start.1
  218.3 135.4 %collective-permute-done.1 = f32[192,8192]{1,0:T(8,128)S(1)} collective-permute-done((f32[192,8192]{1,0:T(8,128)S(1)}, f32[192,8192]{1,0:T(8,128)S(1)}, u32[]{:S(2)}, u32[]{:S(2)}) %collective-permute-start.1) | collective-permute-done | bytes 6291488 | tf_op jit(solution)/shard_map/ppermute | solution.py:18
  353.7 3.3 add.42
  357.0 2.4 collective-permute-start.2
  359.4 0.0 copy-done.5
  359.4 0.6 dynamic-slice
  360.7 0.0 copy-start.3
  360.7 268.3 %collective-permute-done.2 = f32[192,8192]{1,0:T(8,128)} collective-permute-done((f32[192,8192]{1,0:T(8,128)}, f32[192,8192]{1,0:T(8,128)}, u32[]{:S(2)}, u32[]{:S(2)}) %collective-permute-start.2) | collective-permute-done | bytes 6291488 | tf_op jit(solution)/shard_map/ppermute | solution.py:18
  628.9 5.3 add.43
  634.2 0.0 copy-start.2
  634.3 2.6 copy-done.2
  636.9 0.0 copy-done.3
  636.9 0.2 fusion.11
  637.1 5.8 psum.21
  642.9 0.2 dynamic-update-slice
  643.1 21.5 %all-reduce = f32[192]{0:T(256)S(1)} all-reduce(f32[192]{0:T(256)S(1)} %dynamic-update-slice), channel_id=1, replica_groups=mesh['row'=4,'col'=8] {'col'}, use_global_device_ids=true, to_apply=%add | all-reduce | flops 192 | bytes 1536
  664.6 4.0 fusion.6
  668.6 0.0 all-reduce.4.cloned.1.call-update
  668.6 0.2 all-gather.5.cloned.1.call-start
  668.8 2.3 fusion.12
  671.1 63.4 %all-reduce.4.cloned.1.call-done = f32[192,4096]{1,0:T(8,128)} async-done(((f32[192,4096]{1,0:T(8,128)}), f32[192,4096]{1,0:T(8,128)}) %all-reduce.4.cloned.1.call-update) | async-done | bytes 3145744 | tf_op jit(solution)/shard_map/psum | solution.py:27
  734.5 4.4 multiply_convert_fusion
  738.9 30.7 %fusion.19 = f32[192,8192]{1,0:T(8,128)} fusion(bf16[192,4096]{1,0:T(8,128)(2,1)} %multiply_convert_fusion, bf16[8192,4096]{1,0:T(8,128)(2,1)} %param.5), kind=kOutput, calls=%fused_computation.33 | convolution fusion | flops 12884901888 | bytes 74973184 | tf_op jit(solution)/shard_map/dot_general | solution.py:49
  769.6 1.5 collective-permute-start.3
  771.0 0.0 all-gather.5.cloned.1.call-update
  771.1 178.1 %collective-permute-done.3 = f32[192,8192]{1,0:T(8,128)} collective-permute-done((f32[192,8192]{1,0:T(8,128)}, f32[192,8192]{1,0:T(8,128)}, u32[]{:S(2)}, u32[]{:S(2)}) %collective-permute-start.3) | collective-permute-done | bytes 6291488 | tf_op jit(solution)/shard_map/ppermute | solution.py:18
  949.2 5.3 add.47
  954.5 1.6 collective-permute-start.4
  956.0 134.8 %collective-permute-done.4 = f32[192,8192]{1,0:T(8,128)S(1)} collective-permute-done((f32[192,8192]{1,0:T(8,128)S(1)}, f32[192,8192]{1,0:T(8,128)S(1)}, u32[]{:S(2)}, u32[]{:S(2)}) %collective-permute-start.4) | collective-permute-done | bytes 6291488 | tf_op jit(solution)/shard_map/ppermute | solution.py:18
  1090.8 3.2 add.48
  1094.0 2.4 collective-permute-start.5
  1096.4 0.1 dynamic_slice.19
  1096.5 0.0 copy-start.4
  1096.5 0.0 all-gather.5.cloned.1.call-done
  1096.5 5.5 fusion.8
  1102.0 1.3 divide_bitcast_fusion
  1103.2 262.1 %collective-permute-done.5 = f32[192,8192]{1,0:T(8,128)} collective-permute-done((f32[192,8192]{1,0:T(8,128)}, f32[192,8192]{1,0:T(8,128)}, u32[]{:S(2)}, u32[]{:S(2)}) %collective-permute-start.5) | collective-permute-done | bytes 6291488 | tf_op jit(solution)/shard_map/ppermute | solution.py:18
  1365.4 0.0 copy-done.4
  1365.4 1.6 fusion.10
  1367.0 5.8 psum.23
  1372.8 0.2 dynamic-update-slice.1
  1373.0 22.3 %all-reduce.1 = f32[192]{0:T(256)S(1)} all-reduce(f32[192]{0:T(256)S(1)} %dynamic-update-slice.1), channel_id=1, replica_groups=mesh['row'=4,'col'=8] {'col'}, use_global_device_ids=true, to_apply=%add.1 | all-reduce | flops 192 | bytes 1536
  1395.3 0.0 copy-start.6
  1395.3 0.1 dynamic_slice.18
  1395.4 1.6 divide_bitcast_fusion.1
  1397.0 1.2 pad_maximum_fusion
  1398.3 0.0 copy-done.6
  1398.3 0.0 copy-start.1
  1398.3 6.2 fusion.1
  1404.5 0.0 copy-done.1
  (2 shorter events, 0.0 us)
Async XLA Ops:
  8.0 33.7 %copy-start = (bf16[96,4096]{1,0:T(8,128)(2,1)S(1)}, bf16[96,4096]{1,0:T(8,128)(2,1)}, u32[]{:S(2)}) copy-start(bf16[96,4096]{1,0:T(8,128)(2,1)} %param.6) | copy-start | bytes 2359300
  8.0 33.7 %all-gather.3.cloned.1.call-start = ((), (), s32[]{:S(2)}) async-start(), calls=%async_computation | async-start | bytes 3932160 | tf_op jit(solution)/shard_map/all_gather | solution.py:40
  8.7 725.7 %all-reduce.4.cloned.1.call-start = ((), (), s32[]{:S(2)}) async-start(), calls=%async_computation.1 | async-start | bytes 6291456 | tf_op jit(solution)/shard_map/psum | solution.py:27
  75.3 137.9 %collective-permute-start = (f32[192,8192]{1,0:T(8,128)}, f32[192,8192]{1,0:T(8,128)S(1)}, u32[]{:S(2)}, u32[]{:S(2)}) collective-permute-start(f32[192,8192]{1,0:T(8,128)} %fusion.18), channel_id=1, source_target_pairs={{0,1},{1,0},{2,3},{3,2},{4,5},{5,4},{6,7},{7,6},{8,9},{9,8},{10,11... | collective-permute-start | bytes 18874376 | tf_op jit(solution)/shard_map/ppermute | solution.py:18
  216.8 142.6 %copy-start.5 = (u32[32]{0:T(128)S(1)}, u32[32]{0:T(128)}, u32[]{:S(2)}) copy-start(u32[32]{0:T(128)} %constant.48) | copy-start | bytes 388
  216.8 136.9 %collective-permute-start.1 = (f32[192,8192]{1,0:T(8,128)S(1)}, f32[192,8192]{1,0:T(8,128)S(1)}, u32[]{:S(2)}, u32[]{:S(2)}) collective-permute-start(f32[192,8192]{1,0:T(8,128)S(1)} %add.41), channel_id=1, source_target_pairs={{0,2},{1,3},{2,0},{3,1},{4,6},{5,7},{6,4},{7,5},{8,10},{9,11},{10,... | collective-permute-start | bytes 18874376 | tf_op jit(solution)/shard_map/ppermute | solution.py:18
  357.0 272.0 %collective-permute-start.2 = (f32[192,8192]{1,0:T(8,128)}, f32[192,8192]{1,0:T(8,128)}, u32[]{:S(2)}, u32[]{:S(2)}) collective-permute-start(f32[192,8192]{1,0:T(8,128)} %add.42), channel_id=1, source_target_pairs={{0,4},{1,5},{2,6},{3,7},{4,0},{5,1},{6,2},{7,3},{8,12},{9,13},{10,... | collective-permute-start | bytes 18874376 | tf_op jit(solution)/shard_map/ppermute | solution.py:18
  360.7 276.2 %copy-start.3 = (bf16[2,24,8192]{2,1,0:T(8,128)(2,1)S(1)}, bf16[2,24,8192]{2,1,0:T(8,128)(2,1)}, u32[]{:S(2)}) copy-start(bf16[2,24,8192]{2,1,0:T(8,128)(2,1)} %param.8) | copy-start | bytes 2359300
  634.2 2.6 copy-start.2
  668.6 427.9 %all-gather.5.cloned.1.call-start = ((), (), s32[]{:S(2)}) async-start(), calls=%async_computation.2 | async-start | bytes 7077888 | tf_op jit(solution)/shard_map/all_gather | solution.py:39
  769.6 179.6 %collective-permute-start.3 = (f32[192,8192]{1,0:T(8,128)}, f32[192,8192]{1,0:T(8,128)}, u32[]{:S(2)}, u32[]{:S(2)}) collective-permute-start(f32[192,8192]{1,0:T(8,128)} %fusion.19), channel_id=1, source_target_pairs={{0,1},{1,0},{2,3},{3,2},{4,5},{5,4},{6,7},{7,6},{8,9},{9,8},{10,11... | collective-permute-start | bytes 18874376 | tf_op jit(solution)/shard_map/ppermute | solution.py:18
  954.5 136.3 %collective-permute-start.4 = (f32[192,8192]{1,0:T(8,128)S(1)}, f32[192,8192]{1,0:T(8,128)S(1)}, u32[]{:S(2)}, u32[]{:S(2)}) collective-permute-start(f32[192,8192]{1,0:T(8,128)S(1)} %add.47), channel_id=1, source_target_pairs={{0,2},{1,3},{2,0},{3,1},{4,6},{5,7},{6,4},{7,5},{8,10},{9,11},{10,... | collective-permute-start | bytes 18874376 | tf_op jit(solution)/shard_map/ppermute | solution.py:18
  1094.0 271.4 %collective-permute-start.5 = (f32[192,8192]{1,0:T(8,128)}, f32[192,8192]{1,0:T(8,128)}, u32[]{:S(2)}, u32[]{:S(2)}) collective-permute-start(f32[192,8192]{1,0:T(8,128)} %add.48), channel_id=1, source_target_pairs={{0,4},{1,5},{2,6},{3,7},{4,0},{5,1},{6,2},{7,3},{8,12},{9,13},{10,... | collective-permute-start | bytes 18874376 | tf_op jit(solution)/shard_map/ppermute | solution.py:18
  1096.5 268.9 %copy-start.4 = (bf16[2,24,8192]{2,1,0:T(8,128)(2,1)S(1)}, bf16[2,24,8192]{2,1,0:T(8,128)(2,1)}, u32[]{:S(2)}) copy-start(bf16[2,24,8192]{2,1,0:T(8,128)(2,1)} %param.8) | copy-start | bytes 2359300
  1395.3 3.0 copy-start.6
  1398.3 6.3 copy-start.1
Sparse Core Ops, SparseCore 0:
  10.4 31.2 all-gather.2
  668.7 65.6 all-reduce.3
Sparse Core Ops, SparseCore 1:
  771.2 135.9 all-gather.4
